TPU v7x, 32 devices: a whole 2x2x4 slice. The times are simulated.
32 devices in a mesh: dp: 8 (over y, x, core), tensor: 4 (over z).
Axes of the slice: x: 2, y: 2, z: 4, core: 2. Of those that a mesh axis runs over, the one named last changes fastest.
Arguments:
- out_grad: bfloat16 [8, 256, 4096], P('dp', 'tensor'), may hold values from -6 to 6
- out_weight: bfloat16 [4096, 1024], P('dp', 'tensor'), may hold values from -0.1875 to 0.1875
- queries: bfloat16 [8, 256, 1024], P('dp', None, 'tensor'), may hold values from -5 to 5
- keys: bfloat16 [8, 256, 512], P('dp', None, 'tensor'), may hold values from -5 to 5, as said below
- values: bfloat16 [8, 256, 512], P('dp', None, 'tensor'), may hold values from -6 to 6, as said below
- segment_ids: int32 [8, 256], P('dp'), may hold values from 0 to 3, never falling along the last dimension, each value on 1 to 128 neighbouring positions
Outputs:
- d_queries: bfloat16 [8, 256, 1024], P('dp', None, 'tensor')
- d_keys: bfloat16 [8, 256, 512], P('dp', None, 'tensor')
- d_values: bfloat16 [8, 256, 512], P('dp', None, 'tensor')
- d_out_weight: float32 [4096, 1024], P('dp', 'tensor')
Inputs may be any that keep to these rules, and one draw needn't show every extreme that they name: `keys`: column blocks 2 g and 2 g + 1 are equal. `values`: column blocks 2 g and 2 g + 1 are equal.
All inputs are finite; a program needn't handle non-finite values.
Results may differ from a plain program's by a relative error of at most 0.018.
Values may be sent and summed in bfloat16 or wider, within the bound.
A program may use at most 128 MiB of HBM per device.

v0:
```python
import jax
import jax.numpy as jnp
from jax import lax
from jax.sharding import PartitionSpec as P

HD = 128


def from_partner(block, axis, bit):
    count = lax.axis_size(axis)
    route = []
    for low in range(count):
        high = low | 1 << bit
        if high != low and high < count:
            route += [(low, high), (high, low)]
    return lax.ppermute(block, axis, route)


def local(out_grad, out_weight, queries, keys, values, segment_ids):
    scale = HD ** (-0.5)
    grad_local = out_grad[0]
    query_rows = queries[0]
    length = query_rows.shape[0]
    width = query_rows.shape[1]
    heads_here = width // HD
    key_local = keys[0]
    value_local = values[0]
    query_heads = query_rows.reshape(length, heads_here, HD)
    scores = (
        jnp.einsum("qhd,kd->hqk", query_heads, key_local, preferred_element_type=jnp.float32)
        * scale
    )
    segments = segment_ids[0]
    position = jnp.arange(length)
    visible = (segments[:, None] == segments[None, :]) & (position[:, None] >= position[None, :])
    masked = jnp.where(visible[None], scores, -jnp.inf)
    top_score = jnp.max(masked, axis=-1, keepdims=True)
    raw_exp = jnp.exp(masked - top_score)
    attn_prob = raw_exp / jnp.sum(raw_exp, axis=-1, keepdims=True)
    prob_low = attn_prob.astype(jnp.bfloat16)
    attn_out = jnp.einsum(
        "hqk,kd->qhd", prob_low, value_local, preferred_element_type=jnp.float32
    ).astype(jnp.bfloat16)
    flat_out = attn_out.reshape(length, width)
    grad_full = lax.all_gather(grad_local, "tensor", axis=0, tiled=True)
    columns = grad_full
    grad_sum = jnp.dot(
        columns,
        lax.all_gather(out_weight, "dp", axis=0, tiled=True),
        preferred_element_type=jnp.float32,
    )
    columns = grad_full
    weight_rows = lax.psum_scatter(
        lax.dot_general(
            columns, flat_out, (((0,), (0,)), ((), ())), preferred_element_type=jnp.float32
        ).astype(jnp.bfloat16),
        "dp",
        scatter_dimension=0,
        tiled=True,
    ).astype(jnp.float32)
    grad_attn = grad_sum.astype(jnp.bfloat16)
    grad_heads = grad_attn.reshape(length, heads_here, HD)
    deltas = jnp.sum(grad_heads.astype(jnp.float32) * attn_out.astype(jnp.float32), axis=-1)
    grad_values = jnp.einsum(
        "hqk,qhd->kd", prob_low, grad_heads, preferred_element_type=jnp.float32
    )
    grad_prob = jnp.einsum(
        "qhd,kd->hqk", grad_heads, value_local, preferred_element_type=jnp.float32
    )
    grad_score = (attn_prob * (grad_prob - jnp.transpose(deltas)[:, :, None]) * scale).astype(
        jnp.bfloat16
    )
    grad_queries = jnp.einsum(
        "hqk,kd->qhd", grad_score, key_local, preferred_element_type=jnp.float32
    ).astype(jnp.bfloat16)
    grad_keys = jnp.einsum(
        "hqk,qhd->kd", grad_score, query_heads, preferred_element_type=jnp.float32
    )
    partner_keys, partner_values = (
        from_partner(grad_keys.astype(jnp.bfloat16), "tensor", 0).astype(grad_keys.dtype),
        from_partner(grad_values.astype(jnp.bfloat16), "tensor", 0).astype(grad_values.dtype),
    )
    keys_total = (grad_keys + partner_keys).astype(jnp.bfloat16)
    values_total = (grad_values + partner_values).astype(jnp.bfloat16)
    weight_grad = weight_rows / lax.axis_size("dp")
    return (
        grad_queries.reshape(1, length, width),
        keys_total[None],
        values_total[None],
        weight_grad,
    )


def solution(mesh):
    in_specs = (
        P("dp", "tensor", None),
        P("dp", "tensor"),
        P("dp", None, "tensor"),
        P("dp", None, "tensor"),
        P("dp", None, "tensor"),
        P("dp", None),
    )
    out_specs = (
        P("dp", None, "tensor"),
        P("dp", None, "tensor"),
        P("dp", None, "tensor"),
        P("dp", "tensor"),
    )
    return jax.shard_map(local, mesh=mesh, in_specs=in_specs, out_specs=out_specs, check_vma=False)
```

profile of v0, /device:TPU:0, one launch (start us, length us, event | category | flops | bytes accessed | tf_op | source)
XLA Modules:
  0.0 143.6 jit_solution(18421356278678418032)
XLA Ops:
  7.2 0.0 copy-start
  7.2 0.0 all-gather.6.cloned.1.call-start
  7.2 0.7 all-gather.6.cloned.1.call-update
  7.9 0.0 all-gather.4.cloned.1.call-start
  8.0 0.7 all-gather.4.cloned.1.call-update
  8.7 0.0 reduce-scatter.2.cloned.1.call-start
  8.7 0.9 reshape_squeeze.3
  9.7 0.9 fusion.16
  10.5 0.0 copy-done
  10.5 0.3 fusion.55
  10.9 47.4 %all-gather.6.cloned.1.call-done = bf16[1,256,4096]{2,1,0:T(8,128)(2,1)} async-done(((bf16[1,64,4096]{2,1,0:T(8,128)(2,1)}), bf16[1,256,4096]{2,1,0:T(8,128)(2,1)}) %all-gather.6.cloned.1.call-update) | async-done | bytes 2097168 | tf_op jit(solution)/shard_map/all_gather | solution.py:45
  58.3 28.5 %all-gather.4.cloned.1.call-done = bf16[4096,256]{1,0:T(8,128)(2,1)} async-done(((bf16[512,256]{1,0:T(8,128)(2,1)}), bf16[4096,256]{1,0:T(8,128)(2,1)}) %all-gather.4.cloned.1.call-update) | async-done | bytes 2097168 | tf_op jit(solution)/shard_map/all_gather | solution.py:49
  86.8 3.1 %fusion.13 = bf16[256,256]{0,1:T(8,128)(2,1)S(1)} fusion(bf16[4096,256]{1,0:T(8,128)(2,1)} %all-gather.4.cloned.1.call-done, bf16[1,256,4096]{2,1,0:T(8,128)(2,1)} %all-gather.6.cloned.1.call-done), kind=kOutput, calls=%fused_computation.18 | convolution fusion | flops 536936448 | bytes 4325376 | tf_op jit(solution)/shard_map/dot_general | solution.py:47
  89.9 0.0 copy-start.1
  90.0 0.5 multiply_reduce_fusion
  90.5 1.0 copy-done.1
  91.5 2.1 %fusion.1 = bf16[4096,256]{0,1:T(8,128)(2,1)} fusion(bf16[256,256]{0,1:T(8,128)(2,1)S(1)} %bitcast.105, bf16[1,256,4096]{2,1,0:T(8,128)(2,1)S(1)} %copy-done.1), kind=kOutput, calls=%fused_computation.2 | convolution fusion | flops 537919488 | bytes 4325376 | tf_op jit(solution)/shard_map/dot_general | solution.py:54
  93.6 0.0 reduce-scatter.2.cloned.1.call-update
  93.6 0.2 fusion.12
  93.8 0.2 fusion.64
  94.1 1.5 %collective-permute-start = (bf16[256,128]{1,0:T(8,128)(2,1)S(1)}, bf16[256,128]{1,0:T(8,128)(2,1)S(1)}, u32[]{:S(2)}, u32[]{:S(2)}) collective-permute-start(bf16[256,128]{1,0:T(8,128)(2,1)S(1)} %get-tuple-element.12), channel_id=1, source_target_pairs={{0,1},{1,0},{2,3},{3,2},{4,5},{5,4},{6,7},{7,6},{8,9},{9,8},{10,11... | collective-permute-start | bytes 196616 | tf_op jit(solution)/shard_map/ppermute | solution.py:16
  95.6 0.2 convolution_convert_fusion.1
  95.8 0.5 fusion.65
  96.4 0.8 copy.19
  97.1 0.5 collective-permute-start.1
  97.7 0.7 collective-permute-done
  98.4 0.6 fusion.20
  99.0 2.3 %collective-permute-done.1 = bf16[256,128]{1,0:T(8,128)(2,1)S(1)} collective-permute-done((bf16[256,128]{1,0:T(8,128)(2,1)S(1)}, bf16[256,128]{1,0:T(8,128)(2,1)S(1)}, u32[]{:S(2)}, u32[]{:S(2)}) %collective-permute-start.1) | collective-permute-done | bytes 65568 | tf_op jit(solution)/shard_map/ppermute | solution.py:16
  101.4 0.6 fusion.21
  102.0 33.0 %reduce-scatter.2.cloned.1.call-done = bf16[512,256]{0,1:T(8,128)(2,1)} async-done(((bf16[4096,256]{0,1:T(8,128)(2,1)}), bf16[512,256]{0,1:T(8,128)(2,1)}) %reduce-scatter.2.cloned.1.call-update) | async-done | bytes 262160 | tf_op jit(solution)/shard_map/reduce_scatter | solution.py:53
  135.0 1.0 convert_multiply_fusion
  136.0 1.0 copy.20
  (2 shorter events, 0.0 us)
Async XLA Ops:
  7.2 3.4 %copy-start = (bf16[1,256,128]{2,1,0:T(8,128)(2,1)S(1)}, bf16[1,256,128]{2,1,0:T(8,128)(2,1)}, u32[]{:S(2)}) copy-start(bf16[1,256,128]{2,1,0:T(8,128)(2,1)} %param.9) | copy-start | bytes 196612
  7.2 51.1 %all-gather.6.cloned.1.call-start = ((), (), s32[]{:S(2)}) async-start(), calls=%async_computation.3 | async-start | bytes 2621440 | tf_op jit(solution)/shard_map/all_gather | solution.py:45
  7.9 78.9 %all-gather.4.cloned.1.call-start = ((), (), s32[]{:S(2)}) async-start(), calls=%async_computation.1 | async-start | bytes 2359296 | tf_op jit(solution)/shard_map/all_gather | solution.py:49
  8.7 126.3 %reduce-scatter.2.cloned.1.call-start = ((), (), s32[]{:S(2)}) async-start(), calls=%async_computation.2 | async-start | bytes 2359296 | tf_op jit(solution)/shard_map/reduce_scatter | solution.py:53
  10.9 79.1 %copy-start.2 = (bf16[1,256,128]{2,1,0:T(8,128)(2,1)S(1)}, bf16[1,256,128]{2,1,0:T(8,128)(2,1)}, u32[]{:S(2)}) copy-start(bf16[1,256,128]{2,1,0:T(8,128)(2,1)} %param.10) | copy-start | bytes 196612
  89.9 1.6 %copy-start.1 = (bf16[1,256,4096]{2,1,0:T(8,128)(2,1)S(1)}, bf16[1,256,4096]{2,1,0:T(8,128)(2,1)}, u32[]{:S(2)}) copy-start(bf16[1,256,4096]{2,1,0:T(8,128)(2,1)} %all-gather.6.cloned.1.call-done) | copy-start | bytes 6291460
  94.1 4.3 %collective-permute-start = (bf16[256,128]{1,0:T(8,128)(2,1)S(1)}, bf16[256,128]{1,0:T(8,128)(2,1)S(1)}, u32[]{:S(2)}, u32[]{:S(2)}) collective-permute-start(bf16[256,128]{1,0:T(8,128)(2,1)S(1)} %get-tuple-element.12), channel_id=1, source_target_pairs={{0,1},{1,0},{2,3},{3,2},{4,5},{5,4},{6,7},{7,6},{8,9},{9,8},{10,11... | collective-permute-start | bytes 196616 | tf_op jit(solution)/shard_map/ppermute | solution.py:16
  97.1 4.3 %collective-permute-start.1 = (bf16[256,128]{1,0:T(8,128)(2,1)S(1)}, bf16[256,128]{1,0:T(8,128)(2,1)S(1)}, u32[]{:S(2)}, u32[]{:S(2)}) collective-permute-start(bf16[256,128]{1,0:T(8,128)(2,1)S(1)} %get-tuple-element.14), channel_id=1, source_target_pairs={{0,1},{1,0},{2,3},{3,2},{4,5},{5,4},{6,7},{7,6},{8,9},{9,8},{10,11... | collective-permute-start | bytes 196616 | tf_op jit(solution)/shard_map/ppermute | solution.py:16
Sparse Core Ops, SparseCore 0:
  9.6 48.6 all-gather.5
  60.1 26.5 all-gather.3
  93.7 41.2 reduce-scatter.1
where the time goes:
time: 144 us
  waiting for transfers between devices  113 us (78%)
  between operations  13.8 us (10%)
  matrix products  7.24 us (5%)
  local copies, waits for them, and re-layouts  3.77 us (3%)
  other arithmetic  3.15 us (2%)
  starting transfers between devices  2.2 us (2%)
    all_gather x1, waiting for transfers between devices, local(): grad_full = lax.all_gather(grad_local, 'tensor', axis=0, tiled=True)  47.4 us
    reduce_scatter x1, waiting for transfers between devices, local(): lax.psum_scatter(lax.dot_general(columns, flat_out, (((0,), (0,)), ((), (...  33 us
    all_gather x1, waiting for transfers between devices, local(): lax.all_gather(out_weight, 'dp', axis=0, tiled=True)  28.5 us
    dot_general x1, matrix products, local(): jnp.dot(columns, lax.all_gather(out_weight, 'dp', axis=0, tiled=True), pr...  3.15 us
    ppermute x2, waiting for transfers between devices, from_partner(): return lax.ppermute(block, axis, route)  3.08 us
  transfers between devices with their start and end apart: 5, of which 5 were waited for; matrix products, arithmetic and copies ran while one was open for 4% of the time, Pallas kernels for 0%

commit v1 on v0

--- a/solution.py
+++ b/solution.py
@@ -4,6 +4,12 @@
 from jax.sharding import PartitionSpec as P
 
 HD = 128
+
+
+def in_order(tiles, dim):
+    tiles = jnp.moveaxis(tiles, 0, dim)
+    shape = tiles.shape
+    return tiles.reshape(*shape[:dim], shape[dim] * shape[dim + 1], *shape[dim + 2 :])
 
 
 def from_partner(block, axis, bit):
@@ -42,7 +48,14 @@
         "hqk,kd->qhd", prob_low, value_local, preferred_element_type=jnp.float32
     ).astype(jnp.bfloat16)
     flat_out = attn_out.reshape(length, width)
-    grad_full = lax.all_gather(grad_local, "tensor", axis=0, tiled=True)
+    length_2 = lax.axis_size("tensor")
+    upward = [(i, (i + 1) % length_2) for i in range(length_2)]
+    blocks = [grad_local]
+    while len(blocks) < length_2:
+        blocks.append(lax.ppermute(blocks[-1], "tensor", upward))
+    index = lax.axis_index("tensor")
+    blocks = jnp.stack(blocks)[(index - jnp.arange(length_2)) % length_2]
+    grad_full = in_order(blocks, 0)
     columns = grad_full
     grad_sum = jnp.dot(
         columns,

time: 144 us -> 111 us (0.77)
  waiting for transfers between devices: 113 us -> 75.3 us
  starting transfers between devices: 2.2 us -> 5.24 us
  other arithmetic: 3.15 us -> 5.51 us
    all_gather x1 -> x0, waiting for transfers between devices: 47.4 us -> none  [local(): grad_full = lax.all_gather(grad_local, 'tensor', axis=0, tiled=True)]
    ppermute x0 -> x3, waiting for transfers between devices: none -> 40.9 us  [local(): blocks.append(lax.ppermute(blocks[-1], 'tensor', upward))]
    all_gather x1, waiting for transfers between devices: 28.5 us -> 0.02 us  [local(): lax.all_gather(out_weight, 'dp', axis=0, tiled=True)]
    ppermute x0 -> x3, starting transfers between devices: none -> 3.08 us  [local(): blocks.append(lax.ppermute(blocks[-1], 'tensor', upward))]
    gather x0 -> x1, local copies, waits for them, and re-layouts: none -> 2.27 us  [local(): blocks = jnp.stack(blocks)[(index - jnp.arange(length_2)) % length_2]]
    unnamed x8 -> x7, local copies, waits for them, and re-layouts: 2.83 us -> 0.78 us
    another operation x0 -> x1, other arithmetic: none -> 1.57 us  [local(): blocks = jnp.stack(blocks)[(index - jnp.arange(length_2)) % length_2]]
  transfers between devices with their start and end apart: 5 -> 7, of which waited for: 5 -> 6; matrix products, arithmetic and copies ran while one was open for 4% -> 8% of each run, Pallas kernels for 0% -> 0%
where the time goes in v1:
time: 111 us
  waiting for transfers between devices  75.3 us (68%)
  between operations  14.2 us (13%)
  matrix products  6.69 us (6%)
  other arithmetic  5.51 us (5%)
  starting transfers between devices  5.24 us (5%)
  local copies, waits for them, and re-layouts  3.99 us (4%)
    ppermute x3, waiting for transfers between devices, local(): blocks.append(lax.ppermute(blocks[-1], 'tensor', upward))  40.9 us
    reduce_scatter x1, waiting for transfers between devices, local(): lax.psum_scatter(lax.dot_general(columns, flat_out, (((0,), (0,)), ((), (...  32.1 us
    ppermute x3, starting transfers between devices, local(): blocks.append(lax.ppermute(blocks[-1], 'tensor', upward))  3.08 us
    dot_general x1, matrix products, local(): jnp.dot(columns, lax.all_gather(out_weight, 'dp', axis=0, tiled=True), pr...  2.55 us
    gather x1, local copies, waits for them, and re-layouts, local(): blocks = jnp.stack(blocks)[(index - jnp.arange(length_2)) % length_2]  2.27 us
  transfers between devices with their start and end apart: 7, of which 6 were waited for; matrix products, arithmetic and copies ran while one was open for 8% of the time, Pallas kernels for 0%

profile of v1, /device:TPU:0, one launch (start us, length us, event | category | flops | bytes accessed | tf_op | source)
XLA Modules:
  0.0 110.9 jit_solution(935879947387347828)
XLA Ops:
  7.2 0.0 copy-start
  7.2 0.0 all-gather.2.cloned.1.call-start
  7.2 0.7 all-gather.2.cloned.1.call-update
  7.9 0.0 reduce-scatter.2.cloned.1.call-start
  8.0 3.1 %collective-permute-start = (bf16[64,4096]{1,0:T(8,128)(2,1)}, bf16[64,4096]{1,0:T(8,128)(2,1)S(1)}, u32[]{:S(2)}, u32[]{:S(2)}) collective-permute-start(bf16[64,4096]{1,0:T(8,128)(2,1)} %bitcast.105), channel_id=1, source_target_pairs={{0,1},{1,2},{2,3},{3,0},{4,5},{5,6},{6,7},{7,4},{8,9},{9,10},{10,1... | collective-permute-start | bytes 1572872 | tf_op jit(solution)/shard_map/ppermute | solution.py:55
  11.0 14.2 %collective-permute-done = bf16[64,4096]{1,0:T(8,128)(2,1)S(1)} collective-permute-done((bf16[64,4096]{1,0:T(8,128)(2,1)}, bf16[64,4096]{1,0:T(8,128)(2,1)S(1)}, u32[]{:S(2)}, u32[]{:S(2)}) %collective-permute-start) | collective-permute-done | bytes 524320 | tf_op jit(solution)/shard_map/ppermute | solution.py:55
  25.2 14.9 %collective-permute-done.1 = bf16[64,4096]{1,0:T(8,128)(2,1)S(1)} collective-permute-done((bf16[64,4096]{1,0:T(8,128)(2,1)S(1)}, bf16[64,4096]{1,0:T(8,128)(2,1)S(1)}, u32[]{:S(2)}, u32[]{:S(2)}) %collective-permute-start.1) | collective-permute-done | bytes 524320 | tf_op jit(solution)/shard_map/ppermute | solution.py:55
  40.1 0.9 reshape_squeeze.3
  41.1 0.9 fusion.9
  41.9 0.3 fusion.50
  42.3 11.8 %collective-permute-done.2 = bf16[64,4096]{1,0:T(8,128)(2,1)S(1)} collective-permute-done((bf16[64,4096]{1,0:T(8,128)(2,1)S(1)}, bf16[64,4096]{1,0:T(8,128)(2,1)S(1)}, u32[]{:S(2)}, u32[]{:S(2)}) %collective-permute-start.2) | collective-permute-done | bytes 524320 | tf_op jit(solution)/shard_map/ppermute | solution.py:55
  54.1 1.6 %pad_maximum_fusion = bf16[4,64,4096]{2,1,0:T(8,128)(2,1)} fusion(bf16[1,64,4096]{2,1,0:T(8,128)(2,1)S(1)} %bitcast.108, bf16[1,64,4096]{2,1,0:T(8,128)(2,1)S(1)} %bitcast.107, bf16[1,64,4096]{2,1,0:T(8,128)(2,1)S(1)} %bitcast.106, bf16[1,64,4096]{2,1,0:T(8,128)(2,1)S(1)} %copy-done.1), kind=kLoop, calls=%fused_computation.3 | loop fusion | flops 3145728 | bytes 4194304 | tf_op jit(solution)/shard_map/stack | solution.py:57
  55.7 2.3 %gather_fusion = bf16[4,64,4096]{2,1,0:T(8,128)(2,1)S(1)} fusion(bf16[4,64,4096]{2,1,0:T(8,128)(2,1)} %pad_maximum_fusion, s32[1024]{0:T(1024)S(1)} %pad_clamp_fusion), kind=kCustom, calls=%fused_computation | custom fusion | bytes 4194320 | tf_op jit(solution)/shard_map/gather | solution.py:57
  57.9 0.0 all-gather.2.cloned.1.call-done
  58.0 0.0 copy-start.2
  58.0 2.5 %convolution_convert_fusion.3 = bf16[256,256]{0,1:T(8,128)(2,1)S(1)} fusion(bf16[256,4096]{1,0:T(8,128)(2,1)S(1)} %bitcast.102, bf16[4096,256]{1,0:T(8,128)(2,1)} %all-gather.2.cloned.1.call-done), kind=kOutput, calls=%fused_computation.16 | convolution fusion | flops 536936448 | bytes 4325376 | tf_op jit(solution)/shard_map/dot_general | solution.py:60
  60.6 0.5 multiply_reduce_fusion
  61.1 2.1 %convolution_convert_fusion = bf16[4096,256]{1,0:T(8,128)(2,1)} fusion(bf16[256,4096]{1,0:T(8,128)(2,1)S(1)} %bitcast.103, bf16[256,256]{0,1:T(8,128)(2,1)S(1)} %bitcast.109), kind=kOutput, calls=%fused_computation.2 | convolution fusion | flops 537919488 | bytes 4325376 | tf_op jit(solution)/shard_map/dot_general | solution.py:67
  63.2 0.0 reduce-scatter.2.cloned.1.call-update
  63.2 0.2 fusion.8
  63.4 0.2 fusion.59
  63.7 0.1 collective-permute-start.3
  63.7 0.2 convolution_convert_fusion.1
  64.0 0.5 fusion.60
  64.5 0.8 copy.19
  65.3 2.0 %collective-permute-start.4 = (bf16[256,128]{1,0:T(8,128)(2,1)S(1)}, bf16[256,128]{1,0:T(8,128)(2,1)S(1)}, u32[]{:S(2)}, u32[]{:S(2)}) collective-permute-start(bf16[256,128]{1,0:T(8,128)(2,1)S(1)} %get-tuple-element.14), channel_id=1, source_target_pairs={{0,1},{1,0},{2,3},{3,2},{4,5},{5,4},{6,7},{7,6},{8,9},{9,8},{10,11... | collective-permute-start | bytes 196616 | tf_op jit(solution)/shard_map/ppermute | solution.py:22
  67.3 0.7 collective-permute-done.3
  68.0 0.6 fusion.13
  68.6 0.9 collective-permute-done.4
  69.6 0.6 fusion.14
  70.2 32.1 %reduce-scatter.2.cloned.1.call-done = bf16[512,256]{1,0:T(8,128)(2,1)} async-done(((bf16[4096,256]{1,0:T(8,128)(2,1)}), bf16[512,256]{1,0:T(8,128)(2,1)}) %reduce-scatter.2.cloned.1.call-update) | async-done | bytes 262160 | tf_op jit(solution)/shard_map/reduce_scatter | solution.py:66
  102.3 1.8 %convert_multiply_fusion = f32[512,256]{1,0:T(8,128)} fusion(bf16[512,256]{1,0:T(8,128)(2,1)} %reduce-scatter.2.cloned.1.call-done), kind=kLoop, calls=%fused_computation.19 | loop fusion | flops 262144 | bytes 786432 | tf_op jit(solution)/shard_map/div | solution.py:98
  (8 shorter events, 0.0 us)
Async XLA Ops:
  7.2 34.8 %copy-start = (bf16[1,256,128]{2,1,0:T(8,128)(2,1)S(1)}, bf16[1,256,128]{2,1,0:T(8,128)(2,1)}, u32[]{:S(2)}) copy-start(bf16[1,256,128]{2,1,0:T(8,128)(2,1)} %param.9) | copy-start | bytes 196612
  7.2 46.9 %copy-start.1 = (bf16[1,64,4096]{2,1,0:T(8,128)(2,1)S(1)}, bf16[1,64,4096]{2,1,0:T(8,128)(2,1)}, u32[]{:S(2)}) copy-start(bf16[1,64,4096]{2,1,0:T(8,128)(2,1)} %param.6) | copy-start | bytes 1572868
  7.2 50.8 %all-gather.2.cloned.1.call-start = ((), (), s32[]{:S(2)}) async-start(), calls=%async_computation.1 | async-start | bytes 2359296 | tf_op jit(solution)/shard_map/all_gather | solution.py:62
  7.9 94.4 %reduce-scatter.2.cloned.1.call-start = ((), (), s32[]{:S(2)}) async-start(), calls=%async_computation.2 | async-start | bytes 2359296 | tf_op jit(solution)/shard_map/reduce_scatter | solution.py:66
  8.0 17.2 %collective-permute-start = (bf16[64,4096]{1,0:T(8,128)(2,1)}, bf16[64,4096]{1,0:T(8,128)(2,1)S(1)}, u32[]{:S(2)}, u32[]{:S(2)}) collective-permute-start(bf16[64,4096]{1,0:T(8,128)(2,1)} %bitcast.105), channel_id=1, source_target_pairs={{0,1},{1,2},{2,3},{3,0},{4,5},{5,6},{6,7},{7,4},{8,9},{9,10},{10,1... | collective-permute-start | bytes 1572872 | tf_op jit(solution)/shard_map/ppermute | solution.py:55
  25.2 14.9 %collective-permute-start.1 = (bf16[64,4096]{1,0:T(8,128)(2,1)S(1)}, bf16[64,4096]{1,0:T(8,128)(2,1)S(1)}, u32[]{:S(2)}, u32[]{:S(2)}) collective-permute-start(bf16[64,4096]{1,0:T(8,128)(2,1)S(1)} %collective-permute-done), channel_id=1, source_target_pairs={{0,1},{1,2},{2,3},{3,0},{4,5},{5,6},{6,7},{7,4},{8,9},{9,10},{10,1... | collective-permute-start | bytes 1572872 | tf_op jit(solution)/shard_map/ppermute | solution.py:55
  40.1 14.0 %collective-permute-start.2 = (bf16[64,4096]{1,0:T(8,128)(2,1)S(1)}, bf16[64,4096]{1,0:T(8,128)(2,1)S(1)}, u32[]{:S(2)}, u32[]{:S(2)}) collective-permute-start(bf16[64,4096]{1,0:T(8,128)(2,1)S(1)} %collective-permute-done.1), channel_id=1, source_target_pairs={{0,1},{1,2},{2,3},{3,0},{4,5},{5,6},{6,7},{7,4},{8,9},{9,10},{10,1... | collective-permute-start | bytes 1572872 | tf_op jit(solution)/shard_map/ppermute | solution.py:55
  58.0 2.6 %copy-start.2 = (bf16[1,256,128]{2,1,0:T(8,128)(2,1)S(1)}, bf16[1,256,128]{2,1,0:T(8,128)(2,1)}, u32[]{:S(2)}) copy-start(bf16[1,256,128]{2,1,0:T(8,128)(2,1)} %param.10) | copy-start | bytes 196612
  63.7 4.3 %collective-permute-start.3 = (bf16[256,128]{1,0:T(8,128)(2,1)S(1)}, bf16[256,128]{1,0:T(8,128)(2,1)S(1)}, u32[]{:S(2)}, u32[]{:S(2)}) collective-permute-start(bf16[256,128]{1,0:T(8,128)(2,1)S(1)} %get-tuple-element.12), channel_id=1, source_target_pairs={{0,1},{1,0},{2,3},{3,2},{4,5},{5,4},{6,7},{7,6},{8,9},{9,8},{10,11... | collective-permute-start | bytes 196616 | tf_op jit(solution)/shard_map/ppermute | solution.py:22
  65.3 4.3 %collective-permute-start.4 = (bf16[256,128]{1,0:T(8,128)(2,1)S(1)}, bf16[256,128]{1,0:T(8,128)(2,1)S(1)}, u32[]{:S(2)}, u32[]{:S(2)}) collective-permute-start(bf16[256,128]{1,0:T(8,128)(2,1)S(1)} %get-tuple-element.14), channel_id=1, source_target_pairs={{0,1},{1,0},{2,3},{3,2},{4,5},{5,4},{6,7},{7,6},{8,9},{9,8},{10,11... | collective-permute-start | bytes 196616 | tf_op jit(solution)/shard_map/ppermute | solution.py:22
Sparse Core Ops, SparseCore 0:
  9.9 30.5 all-gather.1
  63.3 38.9 reduce-scatter.1
